TPU v7x, 32 devices: a whole 2x2x4 slice. The times are simulated.
32 devices in a mesh: ctx: 8 (over z, y), ch: 4 (over x, core).
Axes of the slice: x: 2, y: 2, z: 4, core: 2. Of those that a mesh axis runs over, the one named last changes fastest.
Arguments:
- features: bfloat16 [3, 1024, 8192], P(None, 'ctx', 'ch'), may hold values from -6 to 6
- grad_rows: bfloat16 [1024, 8192], P(('ctx', 'ch')), may hold values from -6 to 6
- conv_taps: float32 [3, 3, 8192], P(None, None, 'ch'), may hold values from -3.5 to 3.5
- decay_rate: float32 [16, 8192], P(None, 'ch'), may hold values from 0 to 1, as said below
- residue: float32 [16, 8192], P(None, 'ch'), may hold values from -1.5 to 1.5
- skip_gain: float32 [8192], P('ch'), may hold values from -1 to 1
Outputs:
- grad_features: bfloat16 [3, 1024, 8192], P(None, 'ctx', 'ch')
Inputs may be any that keep to these rules, and one draw needn't show every extreme that they name: `decay_rate`: positive decay rates.
All inputs are finite; a program needn't handle non-finite values.
Results may differ from a plain program's by a relative error of at most 0.00125.
Values may be sent and summed in bfloat16 or wider, within the bound.
A program may use at most 128 MiB of HBM per device.

v0:
```python
import math

import jax
import jax.numpy as jnp
from jax import lax
from jax.sharding import PartitionSpec as P


def shifted(block, axis, distance):
    devices = range(lax.axis_size(axis))
    route = [(i - distance, i) for i in devices if i - distance in devices]
    return lax.ppermute(block, axis, route)


def carried_in(value, axis, join, neutral, backward):
    count, mine = (lax.axis_size(axis), lax.axis_index(axis))
    pieces = jax.tree.map(lambda part: lax.all_gather(part, axis), value)
    if backward:
        pieces = jax.tree.map(lambda part: part[::-1], pieces)
        mine = count - 1 - mine
    total = jax.tree.map(
        lambda part, zero: jnp.full_like(part, 0) + jnp.asarray(zero, part.dtype), value, neutral
    )

    def turn(position, total):
        longer = join(total, jax.tree.map(lambda part: part[position], pieces))
        return jax.tree.map(lambda new, old: jnp.where(position < mine, new, old), longer, total)

    return lax.fori_loop(0, count - 1, turn, total)


def local_pass(signal, decay_rate, gain_in, gain_out):
    total_len, width_dev = signal.shape
    block_len = math.gcd(16, total_len)
    block_count = total_len // block_len
    offsets = jnp.arange(block_len, dtype=jnp.float32)
    rates = decay_rate[None]
    decay_in = jnp.exp(-rates * (block_len - 1.0 - offsets)[:, None, None]) * gain_in[None]
    decay_out = jnp.exp(-rates * (offsets + 1.0)[:, None, None]) * gain_out[None]
    kernel = jnp.sum(jnp.exp(-rates * offsets[:, None, None]) * (gain_in * gain_out)[None], axis=1)
    lag_index = (
        jnp.arange(block_len, dtype=jnp.int32)[:, None]
        - jnp.arange(block_len, dtype=jnp.int32)[None, :]
    )
    toeplitz = jnp.where(
        lag_index[:, :, None] >= 0,
        kernel[jnp.maximum(lag_index, 0)],
        jnp.zeros_like(kernel[:1, None]),
    )
    blocks = signal.reshape(block_count, block_len, width_dev)
    local_out = jnp.sum(blocks[:, None, :, :] * toeplitz[None], axis=2)
    block_ends = jnp.sum(blocks[:, :, None, :] * decay_in[None], axis=1)
    block_decay = jnp.exp(-decay_rate * block_len)

    def advance(state_now, entry):
        return (block_decay * state_now + entry, state_now)

    final_state, block_starts = lax.scan(advance, jnp.zeros_like(decay_rate), block_ends)
    return (local_out, block_starts, final_state, decay_out)


def finish(pieces, decay_rate, initial):
    local_out, block_starts, final_state, decay_out = pieces
    block_count, block_len, width_dev = local_out.shape
    anchors = jnp.arange(block_count, dtype=jnp.float32) * block_len
    powers = jnp.exp(-decay_rate[None] * anchors[:, None, None])
    states = block_starts + powers * initial[None]
    result = local_out + jnp.sum(decay_out[None] * states[:, None], axis=2)
    return result.reshape(block_count * block_len, width_dev)


def per_device(features, grad_rows, conv_taps, decay_rate, residue, skip_gain):
    length = features.shape[1]
    rim_rows = conv_taps.shape[1] - 1
    grad_out = lax.all_to_all(grad_rows, "ch", split_axis=1, concat_axis=0, tiled=True)
    last_rows = features[:, length - rim_rows :, :]
    before = shifted(last_rows, "ctx", 1)
    extended = jnp.concatenate([before, features], axis=1)
    featurized = conv_taps[:, 0, None, :] * extended[:, rim_rows : rim_rows + length, :]
    for shift_by in range(1, rim_rows + 1):
        featurized = (
            featurized
            + conv_taps[:, shift_by, None, :]
            * extended[:, rim_rows - shift_by : rim_rows - shift_by + length, :]
        )
    queries = featurized[0]
    keys_feat = featurized[1]
    values_feat = featurized[2]
    gain_in = jnp.sqrt(-jnp.expm1(-2.0 * decay_rate))
    product = keys_feat * values_feat
    forward = local_pass(product, decay_rate, gain_in, residue)
    grad_float = grad_out.astype(jnp.float32)
    grad_conv = grad_float * queries
    backward = local_pass(grad_conv[::-1], decay_rate, jnp.ones_like(decay_rate), residue * gain_in)

    def combine(earlier, later):
        return (
            earlier[0] + later[0],
            jnp.exp(-decay_rate * (length * later[0])) * earlier[1] + later[1],
        )

    single = jnp.ones((), jnp.float32)
    identity = (jnp.zeros((), jnp.float32), jnp.zeros_like(decay_rate))
    state_in = carried_in((single, forward[2]), "ctx", combine, identity, False)[1]
    adjoint_in = carried_in((single, backward[2]), "ctx", combine, identity, True)[1]
    conv_out = finish(forward, decay_rate, state_in) + skip_gain[None] * product
    grad_query = grad_float * conv_out
    grad_product = finish(backward, decay_rate, adjoint_in)[::-1] + skip_gain[None] * grad_conv
    grad_key = grad_product * values_feat
    grad_value = grad_product * keys_feat
    grad_stack = jnp.stack([grad_query, grad_key, grad_value])
    following = shifted(grad_stack[:, :rim_rows, :], "ctx", -1)
    padded = jnp.concatenate([grad_stack, following], axis=1)
    result = conv_taps[:, 0, None, :] * padded[:, 0:length, :]
    for shift_by in range(1, rim_rows + 1):
        result = (
            result + conv_taps[:, shift_by, None, :] * padded[:, shift_by : shift_by + length, :]
        )
    return result.astype(jnp.bfloat16)


def solution(mesh):
    in_specs = (
        P(None, "ctx", "ch"),
        P(("ctx", "ch"), None),
        P(None, None, "ch"),
        P(None, "ch"),
        P(None, "ch"),
        P("ch"),
    )
    out_specs = P(None, "ctx", "ch")
    return jax.shard_map(
        per_device, mesh=mesh, in_specs=in_specs, out_specs=out_specs, check_vma=False
    )
```

profile of v0, /device:TPU:0, one launch (start us, length us, event | category | flops | bytes accessed | tf_op | source)
XLA Modules:
  0.0 231.7 jit_solution(18299917683656548737)
XLA Ops:
  7.5 4.9 %collective-permute-start = (bf16[3,2,2048]{2,1,0:T(2,128)(2,1)S(1)}, bf16[3,2,2048]{2,1,0:T(2,128)(2,1)S(1)}, u32[]{:S(2)}, u32[]{:S(2)}) collective-permute-start(bf16[3,2,2048]{2,1,0:T(2,128)(2,1)S(1)} %slice.41), channel_id=1, source_target_pairs={{0,4},{4,8},{8,12},{12,16},{16,20},{20,24},{24,28},{1,5},{5,9},{9,... | collective-permute-start | bytes 73736 | tf_op jit(solution)/shard_map/ppermute | solution.py:12
  12.4 1.9 copy.18
  14.3 4.1 %all-to-all-start = ((bf16[32,4,2048]{2,0,1:T(8,128)(2,1)}), bf16[32,4,2048]{2,0,1:T(8,128)(2,1)}, u32[]{:S(2)}, u32[]{:S(2)}) async-start(bf16[32,4,2048]{2,0,1:T(8,128)(2,1)} %bitcast.63), calls=%async_computation | async-start | bytes 1048576 | tf_op jit(solution)/shard_map/all_to_all | solution.py:75
  18.5 1.1 fusion.12
  20.4 1.7 multiply_exponential_fusion.3
  22.1 3.9 %fusion.5 = (f32[16,16,2048]{2,1,0:T(8,128)}, f32[16,2048]{1,0:T(8,128)S(1)}, f32[16,16,2048]{2,1,0:T(8,128)}, f32[16,16,2048]{2,1,0:T(8,128)}, f32[16,16,2048]{2,1,0:T(8,128)}) fusion(f32[16]{0:T(128)S(1)} %get-tuple-element.512, f32[16,2048]{1,0:T(8,128)S(1)} %get-tuple-element.503, f32[16,2048]{1,0:T(8,128)S(1)} %get-tuple-element.722, ...), kind=kLoop, calls=%fused_computation.25 | loop fusion | flops 4161536 | bytes 9044096 | tf_op jit(solution)/shard_map/mul | solution.py:39
  26.0 1.5 gather_fusion
  27.5 1.6 broadcast_select_fusion
  30.4 19.5 %all-reduce = f32[8]{0:T(128)S(1)} all-reduce(f32[8]{0:T(128)S(1)} %dynamic-update-slice), channel_id=1, replica_groups=mesh['ctx'=8,'ch'=4] {'ctx'}, use_global_device_ids=true, to_apply=%add | all-reduce | flops 8 | bytes 64
  51.3 3.4 %multiply_add_fusion = f32[3,128,2048]{2,1,0:T(8,128)S(1)} fusion(bf16[3,128,2048]{2,1,0:T(8,128)(2,1)} %param.14, bf16[3,2,2048]{2,1,0:T(2,128)(2,1)} %copy-done.13, f32[3,2048]{1,0:T(4,128)} %get-tuple-element.509, f32[3,2048]{1,0:T(4,128)} %get-tuple-element.510, f32[3,2048]{1,0:T(4,128)} %bitcast.90), kind=kLoop, calls=%fused_computation.22 | loop fusion | flops 11010048 | bytes 4816896 | tf_op jit(solution)/shard_map/add | solution.py:82
  54.7 1.1 slice_multiply_fusion.2
  55.8 2.1 fusion.8
  58.0 8.9 %rev.12 = f32[128,2048]{1,0:T(8,128)} reverse(f32[128,2048]{1,0:T(8,128)} %fusion.8), dimensions={0} | reverse | bytes 2097152 | tf_op jit(solution)/shard_map/rev | solution.py:94
  66.9 14.0 %multiply_reduce_fusion.5 = (f32[8,16,2048]{2,1,0:T(8,128)}, f32[8,16,2048]{2,1,0:T(8,128)}, f32[8,16,2048]{2,1,0:T(8,128)}, f32[8,16,2048]{2,1,0:T(8,128)}) fusion(f32[16,16,2048]{2,1,0:T(8,128)} %broadcast_select_fusion, f32[8,16,2048]{2,1,0:T(8,128)} %bitcast.82, f32[8,16,2048]{2,1,0:T(8,128)} %bitcast.83, f32[16,16,2048]{2,1,0:T(8,128)} %get-tuple-element.500, ...), kind=kLoop, calls=%fused_computation.14 | loop fusion | flops 32505856 | bytes 12582912 | tf_op jit(solution)/shard_map/reduce_sum | solution.py:51
  80.8 1.1 broadcast.129.clone.1
  82.0 13.8 %while.60 = (s32[]{:T(128)}, f32[16,2048]{1,0:T(8,128)S(1)}, f32[8,16,2048]{2,1,0:T(8,128)}, f32[16,2048]{1,0:T(8,128)}, f32[8,16,2048]{2,1,0:T(8,128)}, /*index=5*/s32[]{:T(128)}, s32[]{:T(128)}) while((s32[]{:T(128)}, f32[16,2048]{1,0:T(8,128)S(1)}, f32[8,16,2048]{2,1,0:T(8,128)}, f32[16,2048]{1,0:T(8,128)}, ...), condition=%wide.region_11.12_spmd.clone, body=%wide.region_10.11_spmd.clone.sunk | while | flops 131075 | bytes 787036 | solution.py:58
  84.3 1.0 bitcast_add_fusion.8
  86.1 1.0 bitcast_add_fusion.8
  89.5 1.0 bitcast_add_fusion.8
  91.3 1.0 bitcast_add_fusion.8
  93.0 1.0 bitcast_add_fusion.8
  96.7 1.1 broadcast.129.clone
  97.8 13.8 %while.58 = (s32[]{:T(128)}, f32[16,2048]{1,0:T(8,128)S(1)}, f32[8,16,2048]{2,1,0:T(8,128)}, f32[16,2048]{1,0:T(8,128)}, f32[8,16,2048]{2,1,0:T(8,128)}, /*index=5*/s32[]{:T(128)}, s32[]{:T(128)}) while((s32[]{:T(128)}, f32[16,2048]{1,0:T(8,128)S(1)}, f32[8,16,2048]{2,1,0:T(8,128)}, f32[16,2048]{1,0:T(8,128)}, ...), condition=%wide.region_4.5_spmd.clone, body=%wide.region_3.4_spmd.clone.sunk | while | flops 131075 | bytes 787036 | solution.py:58
  100.2 1.0 bitcast_add_fusion.7
  101.9 1.0 bitcast_add_fusion.7
  107.1 1.0 bitcast_add_fusion.7
  110.6 1.0 bitcast_add_fusion.7
  112.3 22.2 %all-gather.7.cloned.1.call-done = f32[128,2048]{1,0:T(8,128)} async-done(((f32[16,2048]{1,0:T(8,128)}), f32[128,2048]{1,0:T(8,128)}) %all-gather.7.cloned.1.call-update) | async-done | bytes 1048592 | tf_op jit(solution)/shard_map/all_gather | solution.py:17
  134.5 2.3 %rev.14 = f32[8,16,2048]{2,1,0:T(8,128)} reverse(f32[8,16,2048]{2,1,0:T(8,128)} %bitcast.87), dimensions={0} | reverse | bytes 2097152 | tf_op jit(solution)/shard_map/rev | solution.py:19
  136.8 21.1 %while.61 = (s32[]{:T(128)}, f32[16,2048]{1,0:T(8,128)}, s32[]{:T(128)}, f32[8]{0:T(128)S(1)}, f32[16,2048]{1,0:T(8,128)S(1)}, /*index=5*/f32[8,16,2048]{2,1,0:T(8,128)}, s32[]{:T(128)}, f32[1]{0:T(128)}, s32[]{:T(128)}) while((s32[]{:T(128)}, f32[16,2048]{1,0:T(8,128)}, s32[]{:T(128)}, f32[8]{0:T(128)S(1)}, ...), condition=%wide.region_13.14_spmd.clone, body=%wide.region_12.13_spmd.clone.sunk | while | flops 163845 | bytes 524433 | solution.py:29
  138.2 1.6 fusion.16
  141.2 1.7 fusion.16
  144.2 1.7 fusion.16
  147.2 1.7 fusion.16
  150.2 1.7 fusion.16
  153.2 1.7 fusion.16
  156.2 1.7 fusion.16
  157.9 17.6 %all-gather.5.cloned.1.call-done = f32[128,2048]{1,0:T(8,128)} async-done(((f32[16,2048]{1,0:T(8,128)}), f32[128,2048]{1,0:T(8,128)}) %all-gather.5.cloned.1.call-update) | async-done | bytes 1048592 | tf_op jit(solution)/shard_map/all_gather | solution.py:17
  175.5 14.7 %while.59 = (s32[]{:T(128)}, f32[16,2048]{1,0:T(8,128)S(1)}, s32[]{:T(128)}, f32[8]{0:T(128)S(1)}, f32[16,2048]{1,0:T(8,128)S(1)}, /*index=5*/f32[8,16,2048]{2,1,0:T(8,128)}, s32[]{:T(128)}, f32[1]{0:T(128)}, s32[]{:T(128)}) while((s32[]{:T(128)}, f32[16,2048]{1,0:T(8,128)S(1)}, s32[]{:T(128)}, f32[8]{0:T(128)S(1)}, ...), condition=%wide.region_6.7_spmd.clone, body=%wide.region_5.6_spmd.clone.sunk | while | flops 163845 | bytes 524433 | solution.py:29
  190.3 3.0 %multiply_add_fusion.3 = (f32[8,16,2048]{2,1,0:T(8,128)}, f32[8,16,2048]{2,1,0:T(8,128)S(1)}) fusion(f32[8,16,2048]{2,1,0:T(8,128)} %get-tuple-element.359, f32[16,2048]{1,0:T(8,128)S(1)} %get-tuple-element.361, f32[8]{0:T(128)S(1)} %iota_multiply_fusion, f32[16,2048]{1,0:T(8,128)S(1)} %get-tuple-element.748, f32[8,16,2048]{2,1,0:T(8,128)} %get-tuple-element.362, ...), kind=kLoop, calls=%fused_computation.42 | loop fusion | flops 1310720 | bytes 4587552 | tf_op jit(solution)/shard_map/add | solution.py:67
  193.3 4.2 %multiply_reduce_fusion = f32[8,16,2048]{2,1,0:T(8,128)S(1)} fusion(f32[8,16,2048]{2,1,0:T(8,128)S(1)} %get-tuple-element.497, f32[16,16,2048]{2,1,0:T(8,128)S(1)} %copy-done.3), kind=kLoop, calls=%fused_computation.9 | loop fusion | flops 8126464 | bytes 4194304 | tf_op jit(solution)/shard_map/reduce_sum | solution.py:68
  197.5 1.1 add.148
  198.6 8.9 %rev.15 = f32[128,2048]{1,0:T(8,128)} reverse(f32[128,2048]{1,0:T(8,128)} %bitcast.85), dimensions={0} | reverse | bytes 2097152 | tf_op jit(solution)/shard_map/rev | solution.py:108
  207.6 6.2 %multiply_reduce_fusion.3 = f32[8,16,2048]{2,1,0:T(8,128)S(1)} fusion(f32[8,16,2048]{2,1,0:T(8,128)} %get-tuple-element.496, f32[16,16,2048]{2,1,0:T(8,128)} %get-tuple-element.495), kind=kLoop, calls=%fused_computation.12 | loop fusion | flops 8126464 | bytes 4194304 | tf_op jit(solution)/shard_map/reduce_sum | solution.py:68
  214.3 1.4 bitcast_multiply_fusion
  216.1 1.4 collective-permute-start.1
  217.5 4.7 %collective-permute-done.1 = f32[3,2,2048]{2,1,0:T(2,128)S(1)} collective-permute-done((f32[3,2,2048]{2,1,0:T(2,128)S(1)}, f32[3,2,2048]{2,1,0:T(2,128)S(1)}, u32[]{:S(2)}, u32[]{:S(2)}) %collective-permute-start.1) | collective-permute-done | bytes 49184 | tf_op jit(solution)/shard_map/ppermute | solution.py:12
  222.7 2.2 fusion.3
  (102 shorter events, 40.5 us)
Async XLA Ops:
  6.5 15.6 %copy-start.8 = (f32[16,2048]{1,0:T(8,128)S(1)}, f32[16,2048]{1,0:T(8,128)}, u32[]{:S(2)}) copy-start(f32[16,2048]{1,0:T(8,128)} %param.18) | copy-start | bytes 393220
  7.5 43.2 %collective-permute-start = (bf16[3,2,2048]{2,1,0:T(2,128)(2,1)S(1)}, bf16[3,2,2048]{2,1,0:T(2,128)(2,1)S(1)}, u32[]{:S(2)}, u32[]{:S(2)}) collective-permute-start(bf16[3,2,2048]{2,1,0:T(2,128)(2,1)S(1)} %slice.41), channel_id=1, source_target_pairs={{0,4},{4,8},{8,12},{12,16},{16,20},{20,24},{24,28},{1,5},{5,9},{9,... | collective-permute-start | bytes 73736 | tf_op jit(solution)/shard_map/ppermute | solution.py:12
  14.3 41.6 %all-to-all-start = ((bf16[32,4,2048]{2,0,1:T(8,128)(2,1)}), bf16[32,4,2048]{2,0,1:T(8,128)(2,1)}, u32[]{:S(2)}, u32[]{:S(2)}) async-start(bf16[32,4,2048]{2,0,1:T(8,128)(2,1)} %bitcast.63), calls=%async_computation | async-start | bytes 1048576 | tf_op jit(solution)/shard_map/all_to_all | solution.py:75
  18.4 116.1 %all-gather.7.cloned.1.call-start = ((), (), s32[]{:S(2)}) async-start(), calls=%async_computation.2 | async-start | bytes 1179648 | tf_op jit(solution)/shard_map/all_gather | solution.py:17
  27.5 1.6 copy-start.14
  50.7 0.6 copy-start.13
  95.8 0.7 copy-start.1
  96.4 79.1 %all-gather.5.cloned.1.call-start = ((), (), s32[]{:S(2)}) async-start(), calls=%async_computation.1 | async-start | bytes 1179648 | tf_op jit(solution)/shard_map/all_gather | solution.py:17
  111.6 0.7 copy-start
  111.6 63.9 %copy-start.4 = (f32[16,2048]{1,0:T(8,128)S(1)}, f32[16,2048]{1,0:T(8,128)}, u32[]{:S(2)}) copy-start(f32[16,2048]{1,0:T(8,128)} %custom-call.1) | copy-start | bytes 393220
  190.2 3.0 %copy-start.3 = (f32[16,16,2048]{2,1,0:T(8,128)S(1)}, f32[16,16,2048]{2,1,0:T(8,128)}, u32[]{:S(2)}) copy-start(f32[16,16,2048]{2,1,0:T(8,128)} %get-tuple-element.493) | copy-start | bytes 6291460
  193.3 4.2 %copy-start.6 = (f32[8,16,2048]{2,1,0:T(8,128)S(1)}, f32[8,16,2048]{2,1,0:T(8,128)}, u32[]{:S(2)}) copy-start(f32[8,16,2048]{2,1,0:T(8,128)} %get-tuple-element.444) | copy-start | bytes 3145732
  207.5 6.3 %copy-start.5 = (f32[8,16,2048]{2,1,0:T(8,128)S(1)}, f32[8,16,2048]{2,1,0:T(8,128)}, u32[]{:S(2)}) copy-start(f32[8,16,2048]{2,1,0:T(8,128)} %get-tuple-element.443) | copy-start | bytes 3145732
  207.5 6.4 %copy-start.2 = (f32[128,2048]{1,0:T(8,128)S(1)}, f32[128,2048]{1,0:T(8,128)}, u32[]{:S(2)}) copy-start(f32[128,2048]{1,0:T(8,128)} %fusion.8) | copy-start | bytes 3145732
  207.5 6.4 %copy-start.7 = (f32[128,2048]{1,0:T(8,128)S(1)}, f32[128,2048]{1,0:T(8,128)}, u32[]{:S(2)}) copy-start(f32[128,2048]{1,0:T(8,128)} %rev.15) | copy-start | bytes 3145732
  207.6 6.4 %copy-start.12 = (f32[2048]{0:T(1024)S(1)}, f32[2048]{0:T(1024)}, u32[]{:S(2)}) copy-start(f32[2048]{0:T(1024)} %param.19) | copy-start | bytes 24580
  216.1 6.6 %copy-start.9 = (f32[3,2048]{1,0:T(4,128)S(1)}, f32[3,2048]{1,0:T(4,128)}, u32[]{:S(2)}) copy-start(f32[3,2048]{1,0:T(4,128)} %get-tuple-element.509) | copy-start | bytes 73732
  216.1 6.6 %copy-start.10 = (f32[3,2048]{1,0:T(4,128)S(1)}, f32[3,2048]{1,0:T(4,128)}, u32[]{:S(2)}) copy-start(f32[3,2048]{1,0:T(4,128)} %get-tuple-element.510) | copy-start | bytes 73732
  216.1 6.6 %copy-start.11 = (f32[3,1,2048]{2,0,1:T(4,128)S(1)}, f32[3,1,2048]{2,0,1:T(4,128)}, u32[]{:S(2)}) copy-start(f32[3,1,2048]{2,0,1:T(4,128)} %copy.19) | copy-start | bytes 73732
  216.1 6.1 %collective-permute-start.1 = (f32[3,2,2048]{2,1,0:T(2,128)S(1)}, f32[3,2,2048]{2,1,0:T(2,128)S(1)}, u32[]{:S(2)}, u32[]{:S(2)}) collective-permute-start(f32[3,2,2048]{2,1,0:T(2,128)S(1)} %slice.58), channel_id=1, source_target_pairs={{4,0},{8,4},{12,8},{16,12},{20,16},{24,20},{28,24},{5,1},{9,5},{13... | collective-permute-start | bytes 147464 | tf_op jit(solution)/shard_map/ppermute | solution.py:12
Sparse Core Ops, SparseCore 0:
  96.6 37.8 all-gather.6
  136.6 38.8 all-gather.4
where the time goes:
time: 234 us; the launch traced here: 232 us
  other arithmetic  92.9 us (40%)
  waiting for transfers between devices  44.6 us (19%)
  local copies, waits for them, and re-layouts  41 us (18%)
  blocking collectives  19.5 us (8%)
  between operations  13.7 us (6%)
  starting transfers between devices  10.7 us (5%)
  loops' own time  9.21 us (4%)
    all_gather x2, waiting for transfers between devices, carried_in(): pieces = jax.tree.map(lambda part: lax.all_gather(part, axis), value)  39.9 us
    unnamed x1, blocking collectives  19.5 us
    select_n x14, other arithmetic, turn(): jnp.where(position < mine, new, old)  18.3 us
    add x16, other arithmetic, advance(): return (block_decay * state_now + entry, state_now)  16.7 us
    reduce_sum x1, other arithmetic, local_pass(): local_out = jnp.sum(blocks[:, None, :, :] * toeplitz[None], axis=2)  14 us
    dynamic_update_slice x16, other arithmetic, local_pass(): lax.scan(advance, jnp.zeros_like(decay_rate), block_ends)  10.7 us
    reduce_sum x2, other arithmetic, finish(): result = local_out + jnp.sum(decay_out[None] * states[:, None], axis=2)  10.4 us
    another operation x2, loops' own time, carried_in(): return lax.fori_loop(0, count - 1, turn, total)  8.94 us
  transfers between devices with their start and end apart: 5, of which 3 were waited for; matrix products, arithmetic and copies ran while one was open for 23% of the time, Pallas kernels for 0%

commit v1 on v0

v1 whole, which is shorter than its diff:
```python
import functools

import jax
import jax.numpy as jnp
from jax import lax
from jax.experimental import pallas as pl
from jax.experimental.pallas import tpu as pltpu
from jax.sharding import PartitionSpec as P

LANES = 128
SEGS = 8


def one_minus_exp(x):
    series = jnp.ones_like(x)
    for k in range(10, 1, -1):
        series = 1.0 - x * (1.0 / k) * series
    return jnp.where(x < 0.5, x * series, 1.0 - jnp.exp(-x))


def kernel(
    n_ctx,
    n_ch,
    features,
    rows,
    taps,
    rates,
    residue,
    skip,
    out,
    x32,
    grads,
    g32,
    decay,
    seg_decay,
    dev_decay,
    weight,
    short,
    keys,
    values,
    gconv,
    starts,
    partial,
    carry,
    sent,
    landed,
    halo_out,
    halo_in,
    stream,
    rim_out,
    rim_in,
    placed,
    own_sem,
    rows_send,
    rows_recv,
    halo_send,
    halo_recv,
    carry_send,
    carry_recv,
    rim_send,
    rim_recv,
):
    me, mine = lax.axis_index("ctx"), lax.axis_index("ch")
    length, width = features.shape[1], features.shape[2]
    modes = rates.shape[0]
    tiles = width // LANES
    seg = length // SEGS
    piece = rows.shape[0]
    rounds = sent.shape[1]
    group = rim_send.shape[0]
    per = tiles // group

    def lanes(c):
        return pl.ds(pl.multiple_of(c * LANES, LANES), LANES)

    def each(body):
        def step(c, _):
            body(c)
            return 0

        lax.fori_loop(0, tiles, step, 0)

    def wide(row):
        return jnp.broadcast_to(row, (SEGS, LANES))

    place = lax.broadcasted_iota(jnp.int32, (SEGS, LANES), 0)

    barrier = pltpu.get_barrier_semaphore()
    for o in range(1, n_ch):
        pl.semaphore_signal(
            barrier, inc=1, device_id=(me, lax.rem(mine + o, n_ch)), device_id_type=pl.DeviceIdType.MESH
        )
    partners = n_ch - 1
    for k in range(rounds):
        for step in (2**k, -(2**k)):
            there = jnp.logical_and(me + step >= 0, me + step < n_ctx)

            @pl.when(there)
            def _():
                pl.semaphore_signal(
                    barrier, inc=1, device_id=(me + step, mine), device_id_type=pl.DeviceIdType.MESH
                )

            partners = partners + there.astype(jnp.int32)

    def stage(c):
        halo_out[c, 6:8, :] = jnp.zeros((2, LANES), jnp.float32)
        for x in range(3):
            tail = features[x, length - 16 : length, lanes(c)].astype(jnp.float32)
            halo_out[c, 2 * x : 2 * x + 2, :] = tail[14:16]

    each(stage)
    pl.semaphore_wait(barrier, partners)

    halo = pltpu.make_async_remote_copy(
        src_ref=halo_out,
        dst_ref=halo_in,
        send_sem=halo_send,
        recv_sem=halo_recv,
        device_id=(jnp.minimum(me + 1, n_ctx - 1), mine),
        device_id_type=pl.DeviceIdType.MESH,
    )

    @pl.when(me < n_ctx - 1)
    def _():
        halo.start()

    row_copies = []
    spot = pl.ds(pl.multiple_of(mine * piece, piece), piece)
    for o in range(1, n_ch):
        to = lax.rem(mine + o, n_ch)
        row_copies.append(
            pltpu.make_async_remote_copy(
                src_ref=rows.at[:, pl.ds(pl.multiple_of(to * width, LANES), width)],
                dst_ref=grads.at[spot, :],
                send_sem=rows_send.at[o - 1],
                recv_sem=rows_recv.at[o - 1],
                device_id=(me, to),
                device_id_type=pl.DeviceIdType.MESH,
            )
        )
    for copy in row_copies:
        copy.start()
    own = pltpu.make_async_copy(
        rows.at[:, pl.ds(pl.multiple_of(mine * width, LANES), width)], grads.at[spot, :], own_sem
    )
    own.start()

    def prepare(c):
        for x in range(3):
            x32[x, c, 8 : 8 + length, :] = features[x, :, lanes(c)].astype(jnp.float32)
        rate = rates[:, lanes(c)]
        a = jnp.exp(-rate)
        w = residue[:, lanes(c)] * jnp.sqrt(one_minus_exp(2.0 * rate))
        decay[c] = a
        seg_decay[c] = jnp.exp(rate * (-float(seg)))
        dev_decay[c] = jnp.exp(rate * (-float(length)))
        power = w
        for k in range(seg):
            tap = jnp.sum(power, axis=0, keepdims=True)
            if k == 0:
                tap = tap + skip[:, lanes(c)]
            short[c, k : k + 1, :] = tap
            power = power * a
            if k == 0:
                weight[c] = power
        carry[0, c] = jnp.zeros((modes, LANES), jnp.float32)
        carry[1, c] = jnp.zeros((modes, LANES), jnp.float32)

    each(prepare)

    @pl.when(me > 0)
    def _():
        halo.wait_recv()

    @pl.when(me == 0)
    def _():
        halo_in[...] = jnp.zeros(halo_in.shape, jnp.float32)

    def featurized(x, c):
        held = [x32[x, c, pl.ds(8 + j, SEGS, stride=seg), :] for j in range(-2, seg)]
        t = [wide(taps[x, j : j + 1, lanes(c)]) for j in range(3)]
        return [t[0] * held[j + 2] + t[1] * held[j + 1] + t[2] * held[j] for j in range(seg)]

    def ends(signal, c, back):
        order = range(seg - 1, -1, -1) if back else range(seg)
        d = 1 if back else 0
        for low in range(0, modes, 16):
            picked = range(low, min(low + 16, modes))
            a = [wide(decay[c, m : m + 1, :]) for m in picked]
            e = None
            for j in order:
                s = signal[j]
                e = [s] * len(a) if e is None else [a[i] * e[i] + s for i in range(len(a))]
            for i, m in enumerate(picked):
                total = e[i]
                b = wide(seg_decay[c, m : m + 1, :])
                for k in (1, 2, 4):
                    inside = place < SEGS - k if back else place >= k
                    moved = pltpu.roll(total, SEGS - k if back else k, 0)
                    total = total + jnp.where(inside, b, 0.0) * moved
                    b = b * b
                inside = place < SEGS - 1 if back else place >= 1
                moved = pltpu.roll(total, SEGS - 1 if back else 1, 0)
                starts[d, c, m] = jnp.where(inside, moved, 0.0)
                last = total[0:1] if back else total[SEGS - 1 : SEGS]
                sent[d, 0, c, m : m + 1, :] = last

    def reach(d, k):
        return me + 2**k < n_ctx if d == 0 else me >= 2**k

    def comes(d, k):
        return me >= 2**k if d == 0 else me + 2**k < n_ctx

    def carry_copy(d, k):
        to = me + 2**k if d == 0 else me - 2**k
        return pltpu.make_async_remote_copy(
            src_ref=sent.at[d, k],
            dst_ref=landed.at[d, k],
            send_sem=carry_send.at[d, k],
            recv_sem=carry_recv.at[d, k],
            device_id=(jnp.clip(to, 0, n_ctx - 1), mine),
            device_id_type=pl.DeviceIdType.MESH,
        )

    def send(d, k):
        @pl.when(reach(d, k))
        def _():
            carry_copy(d, k).start()

    def take(d, k):
        @pl.when(comes(d, k))
        def _():
            carry_copy(d, k).wait_recv()

            def add(c):
                arrived = landed[d, k, c]
                if k:
                    arrived = arrived * jnp.exp(rates[:, lanes(c)] * (-float(length * (2**k - 1))))
                carry[d, c] = carry[d, c] + arrived

            each(add)

        if k + 1 < rounds:

            @pl.when(reach(d, k + 1))
            def _():
                def join(c):
                    sent[d, k + 1, c] = sent[d, 0, c] + dev_decay[c] * carry[d, c]

                each(join)
                carry_copy(d, k + 1).start()

    def forward_ends(c):
        for x in range(3):
            x32[x, c, 6:8, :] = halo_in[c, 2 * x : 2 * x + 2, :]
        k_now = featurized(1, c)
        v_now = featurized(2, c)
        for j in range(seg):
            keys[c, j] = k_now[j]
            values[c, j] = v_now[j]
        ends([k_now[j] * v_now[j] for j in range(seg)], c, False)

    each(forward_ends)
    if rounds:
        send(0, 0)

    own.wait()
    for copy in row_copies:
        copy.wait()

    def backward_ends(c):
        g32[c] = grads[:, lanes(c)].astype(jnp.float32)
        q_now = featurized(0, c)
        signal = []
        for j in range(seg):
            now = q_now[j] * g32[c, pl.ds(j, SEGS, stride=seg), :]
            gconv[c, j] = now
            signal.append(now)
        ends(signal, c, True)

    each(backward_ends)
    if rounds:
        send(1, 0)
        take(0, 0)

    def forward_short(c):
        h = [wide(short[c, k : k + 1, :]) for k in range(seg)]
        p = [keys[c, j] * values[c, j] for j in range(seg)]
        for j in range(seg):
            total = h[0] * p[j]
            for k in range(1, j + 1):
                total = total + h[k] * p[j - k]
            partial[0, c, j] = total

    each(forward_short)
    if rounds:
        take(1, 0)
    if rounds > 1:
        take(0, 1)

    def backward_short(c):
        h = [wide(short[c, k : k + 1, :]) for k in range(seg)]
        p = [gconv[c, j] for j in range(seg)]
        for j in range(seg):
            total = h[0] * p[j]
            for k in range(1, seg - j):
                total = total + h[k] * p[j + k]
            partial[1, c, j] = total

    each(backward_short)
    if rounds > 1:
        take(1, 1)
    for k in range(2, rounds):
        take(0, k)
        if k + 1 < rounds:
            take(1, k)

    def complete(c, d):
        a = [wide(decay[c, m : m + 1, :]) for m in range(modes)]
        y = []
        count = (SEGS - 1 - place if d else place).astype(jnp.float32) * (-float(seg))
        for m in range(modes):
            entering = jnp.exp(wide(rates[m : m + 1, lanes(c)]) * count)
            state = starts[d, c, m] + entering * wide(carry[d, c, m : m + 1, :])
            y.append(wide(weight[c, m : m + 1, :]) * state)
        result = [None] * seg
        order = range(seg - 1, -1, -1) if d else range(seg)
        for step, j in enumerate(order):
            total = partial[d, c, j]
            if step:
                y = [y[m] * a[m] for m in range(modes)]
            for m in range(modes):
                total = total + y[m]
            result[j] = total
        return result

    def forward_finish(c):
        conv = complete(c, 0)
        for j in range(seg):
            stream[0, c, j] = conv[j] * g32[c, pl.ds(j, SEGS, stride=seg), :]

    each(forward_finish)
    if rounds > 2:
        take(1, rounds - 1)

    def rim_copy(g):
        some = pl.ds(g * per, per)
        return pltpu.make_async_remote_copy(
            src_ref=rim_out.at[some],
            dst_ref=rim_in.at[some],
            send_sem=rim_send.at[g],
            recv_sem=rim_recv.at[g],
            device_id=(jnp.maximum(me - 1, 0), mine),
            device_id_type=pl.DeviceIdType.MESH,
        )

    def backward_finish(c):
        prod = complete(c, 1)
        for j in range(seg):
            stream[1, c, j] = prod[j] * values[c, j]
            stream[2, c, j] = prod[j] * keys[c, j]
        rim_out[c, 6:8, :] = jnp.zeros((2, LANES), jnp.float32)
        for x in range(3):
            for r in range(2):
                rim_out[c, 2 * x + r : 2 * x + r + 1, :] = stream[x, c, r, 0:1, :]

    def finish_group(g, _):
        def one(i, _):
            backward_finish(g * per + i)
            return 0

        lax.fori_loop(0, per, one, 0)

        @pl.when(me > 0)
        def _():
            rim_copy(g).start()

        return 0

    lax.fori_loop(0, group, finish_group, 0)

    @pl.when(me == n_ctx - 1)
    def _():
        rim_in[...] = jnp.zeros(rim_in.shape, jnp.float32)

    def last_taps(c):
        for x in range(3):
            t = [wide(taps[x, j : j + 1, lanes(c)]) for j in range(3)]
            g = [stream[x, c, j] for j in range(seg)]
            for r in range(2):
                moved = pltpu.roll(g[r], SEGS - 1, 0)
                g.append(jnp.where(place == SEGS - 1, wide(rim_in[c, 2 * x + r : 2 * x + r + 1, :]), moved))
            for j in range(seg):
                placed[x, pl.ds(j, SEGS, stride=seg), :] = t[0] * g[j] + t[1] * g[j + 1] + t[2] * g[j + 2]
            out[x, :, lanes(c)] = placed[x].astype(out.dtype)

    def output_group(g, _):
        @pl.when(me < n_ctx - 1)
        def _():
            rim_copy(g).wait_recv()

        def one(i, _):
            last_taps(g * per + i)
            return 0

        lax.fori_loop(0, per, one, 0)
        return 0

    lax.fori_loop(0, group, output_group, 0)

    @pl.when(me < n_ctx - 1)
    def _():
        halo.wait_send()

    for d in range(2):
        for k in range(rounds):

            @pl.when(reach(d, k))
            def _():
                carry_copy(d, k).wait_send()

    @pl.when(me > 0)
    def _():
        def drain(g, _):
            rim_copy(g).wait_send()
            return 0

        lax.fori_loop(0, group, drain, 0)


def per_device(n_ctx, n_ch, features, grad_rows, conv_taps, decay_rate, residue, skip_gain):
    _, length, width = features.shape
    modes = decay_rate.shape[0]
    tiles = width // LANES
    seg = length // SEGS
    rounds = (n_ctx - 1).bit_length()
    group = 4 if tiles % 4 == 0 else 1
    f32 = jnp.float32
    dma = pltpu.SemaphoreType.DMA
    vmem = pl.BlockSpec(memory_space=pltpu.VMEM)
    table = pltpu.VMEM((tiles, modes, LANES), f32)
    tokens = pltpu.VMEM((tiles, seg, SEGS, LANES), f32)
    edge = pltpu.VMEM((tiles, 8, LANES), f32)
    return pl.pallas_call(
        functools.partial(kernel, n_ctx, n_ch),
        out_shape=jax.ShapeDtypeStruct(features.shape, jnp.bfloat16),
        in_specs=[vmem] * 6,
        out_specs=vmem,
        scratch_shapes=[
            pltpu.VMEM((3, tiles, 8 + length, LANES), f32),
            pltpu.VMEM((length, width), jnp.bfloat16),
            pltpu.VMEM((tiles, length, LANES), f32),
            table,
            table,
            table,
            table,
            pltpu.VMEM((tiles, seg, LANES), f32),
            tokens,
            tokens,
            tokens,
            pltpu.VMEM((2, tiles, modes, SEGS, LANES), f32),
            pltpu.VMEM((2, tiles, seg, SEGS, LANES), f32),
            pltpu.VMEM((2, tiles, modes, LANES), f32),
            pltpu.VMEM((2, rounds, tiles, modes, LANES), f32),
            pltpu.VMEM((2, rounds, tiles, modes, LANES), f32),
            edge,
            edge,
            pltpu.VMEM((3, tiles, seg, SEGS, LANES), f32),
            edge,
            edge,
            pltpu.VMEM((3, length, LANES), f32),
            dma,
            dma((n_ch - 1,)),
            dma((n_ch - 1,)),
            dma,
            dma,
            dma((2, rounds)),
            dma((2, rounds)),
            dma((group,)),
            dma((group,)),
        ],
        compiler_params=pltpu.CompilerParams(
            collective_id=0, has_side_effects=True, vmem_limit_bytes=48 * 1024 * 1024
        ),
    )(features, grad_rows, conv_taps, decay_rate, residue, skip_gain[None])


def solution(mesh):
    in_specs = (
        P(None, "ctx", "ch"),
        P(("ctx", "ch"), None),
        P(None, None, "ch"),
        P(None, "ch"),
        P(None, "ch"),
        P("ch"),
    )
    body = functools.partial(per_device, mesh.shape["ctx"], mesh.shape["ch"])
    return jax.shard_map(
        body, mesh=mesh, in_specs=in_specs, out_specs=P(None, "ctx", "ch"), check_vma=False
    )
```

time: 234 us -> 42.5 us (0.18)
  other arithmetic: 92.9 us -> 0 us
  waiting for transfers between devices: 44.6 us -> 0 us
  Pallas kernels: 0 us -> 35.2 us
  local copies, waits for them, and re-layouts: 41 us -> 6.99 us
  blocking collectives: 19.5 us -> 0 us
  between operations: 13.7 us -> 0.02 us
  starting transfers between devices: 10.7 us -> 0 us
  loops' own time: 9.21 us -> 0 us
    all_gather x2 -> x0, waiting for transfers between devices: 39.9 us -> none  [carried_in(): pieces = jax.tree.map(lambda part: lax.all_gather(part, axis), value)]
    pallas_call x0 -> x1, Pallas kernels: none -> 35.2 us  [per_device(): pl.pallas_call(functools.partial(kernel, n_ctx, n_ch), out_shape=jax.Shap...]
    reduce_sum x3 -> x0, other arithmetic: 24.4 us -> none  [the longest x1 14 us: local_pass(): local_out = jnp.sum(blocks[:, None, :, :] * toeplitz[None], axis=2)]
    add x20 -> x0, other arithmetic: 24.4 us -> none  [the longest x16 16.7 us: advance(): return (block_decay * state_now + entry, state_now)]
    rev x4 -> x0, local copies, waits for them, and re-layouts: 20.3 us -> none  [the longest x1 8.94 us: per_device(): finish(backward, decay_rate, adjoint_in)[::-1] + skip_gain[None] * grad_conv]
    select_n x15 -> x0, other arithmetic: 19.9 us -> none  [the longest x14 18.3 us: turn(): jnp.where(position < mine, new, old)]
    unnamed x1 -> x0, blocking collectives: 19.5 us -> none
    dynamic_update_slice x16 -> x0, other arithmetic: 10.7 us -> none  [local_pass(): lax.scan(advance, jnp.zeros_like(decay_rate), block_ends)]
  transfers between devices with their start and end apart: 5 -> 0, of which waited for: 3 -> 0; matrix products, arithmetic and copies ran while one was open for 23% -> 0% of each run, Pallas kernels for 0% -> 0%
where the time goes in v1:
time: 42.5 us; the launch traced here: 42.2 us
  Pallas kernels  35.2 us (83%)
  local copies, waits for them, and re-layouts  6.99 us (16%)
    pallas_call x1, Pallas kernels, per_device(): pl.pallas_call(functools.partial(kernel, n_ctx, n_ch), out_shape=jax.Shap...  35.2 us
    unnamed x13, local copies, waits for them, and re-layouts  6.99 us

profile of v1, /device:TPU:0, one launch (start us, length us, event | category | flops | bytes accessed | tf_op | source)
XLA Modules:
  0.0 42.2 jit_solution(13452174676252488935)
XLA Ops:
  0.0 0.0 copy-start
  0.0 1.4 %copy-done = bf16[3,128,2048]{2,1,0:T(8,128)(2,1)S(1)} copy-done((bf16[3,128,2048]{2,1,0:T(8,128)(2,1)S(1)}, bf16[3,128,2048]{2,1,0:T(8,128)(2,1)}, u32[]{:S(2)}) %copy-start) | copy-done | bytes 1572888
  1.4 0.0 copy-start.1
  1.4 1.0 %copy-done.1 = bf16[32,8192]{1,0:T(8,128)(2,1)S(1)} copy-done((bf16[32,8192]{1,0:T(8,128)(2,1)S(1)}, bf16[32,8192]{1,0:T(8,128)(2,1)}, u32[]{:S(2)}) %copy-start.1) | copy-done | bytes 524312
  2.5 0.0 copy-start.2
  2.5 0.9 %copy-done.2 = f32[16,2048]{1,0:T(8,128)S(1)} copy-done((f32[16,2048]{1,0:T(8,128)S(1)}, f32[16,2048]{1,0:T(8,128)}, u32[]{:S(2)}) %copy-start.2) | copy-done | bytes 131096
  3.4 0.0 copy-start.3
  3.4 0.9 %copy-done.3 = f32[16,2048]{1,0:T(8,128)S(1)} copy-done((f32[16,2048]{1,0:T(8,128)S(1)}, f32[16,2048]{1,0:T(8,128)}, u32[]{:S(2)}) %copy-start.3) | copy-done | bytes 131096
  4.3 0.0 copy-start.4
  4.3 0.9 %copy-done.4 = f32[3,3,2048]{2,1,0:T(4,128)S(1)} copy-done((f32[3,3,2048]{2,1,0:T(4,128)S(1)}, f32[3,3,2048]{2,1,0:T(4,128)}, u32[]{:S(2)}) %copy-start.4) | copy-done | bytes 73752
  5.2 0.0 copy-start.5
  5.2 0.7 %copy-done.5 = f32[2048]{0:T(1024)S(1)} copy-done((f32[2048]{0:T(1024)S(1)}, f32[2048]{0:T(1024)}, u32[]{:S(2)}) %copy-start.5) | copy-done | bytes 8216
  5.9 35.2 %shard_map.64 = bf16[3,128,2048]{2,1,0:T(8,128)(2,1)S(1)} custom-call(bf16[3,128,2048]{2,1,0:T(8,128)(2,1)S(1)} %copy-done, bf16[32,8192]{1,0:T(8,128)(2,1)S(1)} %copy-done.1, f32[3,3,2048]{2,1,0:T(4,128)S(1)} %copy-done.4, f32[16,2048]{1,0:T(8,128)S(1)} %copy-done.2, f32[16,2048]{1,0:T(8,128)S(1)} %copy-done.3, f32[1,2048]{1,0:T(1,128)S(1)} %bitcast.1), custom_call_target="tpu_custom_call" | custom-call | tf_op jit(solution)/shard_map/pallas_call | solution.py:445
  41.0 1.1 %copy.8 = bf16[3,128,2048]{2,1,0:T(8,128)(2,1)} copy(bf16[3,128,2048]{2,1,0:T(8,128)(2,1)S(1)} %shard_map.64) | data formatting | bytes 3145728
Async XLA Ops:
  0.0 1.4 %copy-start = (bf16[3,128,2048]{2,1,0:T(8,128)(2,1)S(1)}, bf16[3,128,2048]{2,1,0:T(8,128)(2,1)}, u32[]{:S(2)}) copy-start(bf16[3,128,2048]{2,1,0:T(8,128)(2,1)} %features.1) | copy-start | bytes 4718596
  1.4 1.0 %copy-start.1 = (bf16[32,8192]{1,0:T(8,128)(2,1)S(1)}, bf16[32,8192]{1,0:T(8,128)(2,1)}, u32[]{:S(2)}) copy-start(bf16[32,8192]{1,0:T(8,128)(2,1)} %rows.1) | copy-start | bytes 1572868
  2.5 0.9 %copy-start.2 = (f32[16,2048]{1,0:T(8,128)S(1)}, f32[16,2048]{1,0:T(8,128)}, u32[]{:S(2)}) copy-start(f32[16,2048]{1,0:T(8,128)} %rates.1) | copy-start | bytes 393220
  3.4 0.9 %copy-start.3 = (f32[16,2048]{1,0:T(8,128)S(1)}, f32[16,2048]{1,0:T(8,128)}, u32[]{:S(2)}) copy-start(f32[16,2048]{1,0:T(8,128)} %residue.1) | copy-start | bytes 393220
  4.3 0.9 %copy-start.4 = (f32[3,3,2048]{2,1,0:T(4,128)S(1)}, f32[3,3,2048]{2,1,0:T(4,128)}, u32[]{:S(2)}) copy-start(f32[3,3,2048]{2,1,0:T(4,128)} %taps.1) | copy-start | bytes 221188
  5.2 0.7 %copy-start.5 = (f32[2048]{0:T(1024)S(1)}, f32[2048]{0:T(1024)}, u32[]{:S(2)}) copy-start(f32[2048]{0:T(1024)} %param.11) | copy-start | bytes 24580

commit v2 on v1

--- a/solution.py
+++ b/solution.py
@@ -21,13 +21,18 @@
 def kernel(
     n_ctx,
     n_ch,
+    features_hbm,
+    rows,
+    taps_hbm,
+    rates_hbm,
+    residue_hbm,
+    skip_hbm,
+    out,
     features,
-    rows,
     taps,
     rates,
     residue,
     skip,
-    out,
     x32,
     grads,
     g32,
@@ -50,6 +55,7 @@
     rim_out,
     rim_in,
     placed,
+    load_sem,
     own_sem,
     rows_send,
     rows_recv,
@@ -73,17 +79,38 @@
     def lanes(c):
         return pl.ds(pl.multiple_of(c * LANES, LANES), LANES)
 
+    def loop(count, body, first=0):
+        def step(i, _):
+            body(first + i)
+            return 0
+
+        lax.fori_loop(0, count, step, 0)
+
     def each(body):
-        def step(c, _):
-            body(c)
-            return 0
-
-        lax.fori_loop(0, tiles, step, 0)
+        loop(tiles, body)
+
+    def within(g, body):
+        loop(per, body, g * per)
 
     def wide(row):
         return jnp.broadcast_to(row, (SEGS, LANES))
 
     place = lax.broadcasted_iota(jnp.int32, (SEGS, LANES), 0)
+
+    loads = [
+        pltpu.make_async_copy(far, near, load_sem.at[i])
+        for i, (far, near) in enumerate(
+            (
+                (features_hbm, features),
+                (rates_hbm, rates),
+                (taps_hbm, taps),
+                (residue_hbm, residue),
+                (skip_hbm, skip),
+            )
+        )
+    ]
+    for load in loads:
+        load.start()
 
     barrier = pltpu.get_barrier_semaphore()
     for o in range(1, n_ch):
@@ -103,27 +130,7 @@
 
             partners = partners + there.astype(jnp.int32)
 
-    def stage(c):
-        halo_out[c, 6:8, :] = jnp.zeros((2, LANES), jnp.float32)
-        for x in range(3):
-            tail = features[x, length - 16 : length, lanes(c)].astype(jnp.float32)
-            halo_out[c, 2 * x : 2 * x + 2, :] = tail[14:16]
-
-    each(stage)
     pl.semaphore_wait(barrier, partners)
-
-    halo = pltpu.make_async_remote_copy(
-        src_ref=halo_out,
-        dst_ref=halo_in,
-        send_sem=halo_send,
-        recv_sem=halo_recv,
-        device_id=(jnp.minimum(me + 1, n_ctx - 1), mine),
-        device_id_type=pl.DeviceIdType.MESH,
-    )
-
-    @pl.when(me < n_ctx - 1)
-    def _():
-        halo.start()
 
     row_copies = []
     spot = pl.ds(pl.multiple_of(mine * piece, piece), piece)
@@ -146,16 +153,41 @@
     )
     own.start()
 
+    def stage(c):
+        halo_out[c, 6:8, :] = jnp.zeros((2, LANES), jnp.float32)
+        for x in range(3):
+            tail = features[x, length - 16 : length, lanes(c)].astype(jnp.float32)
+            halo_out[c, 2 * x : 2 * x + 2, :] = tail[14:16]
+
+    loads[0].wait()
+    each(stage)
+
+    halo = pltpu.make_async_remote_copy(
+        src_ref=halo_out,
+        dst_ref=halo_in,
+        send_sem=halo_send,
+        recv_sem=halo_recv,
+        device_id=(jnp.minimum(me + 1, n_ctx - 1), mine),
+        device_id_type=pl.DeviceIdType.MESH,
+    )
+
+    @pl.when(me < n_ctx - 1)
+    def _():
+        halo.start()
+
     def prepare(c):
         for x in range(3):
             x32[x, c, 8 : 8 + length, :] = features[x, :, lanes(c)].astype(jnp.float32)
         rate = rates[:, lanes(c)]
-        a = jnp.exp(-rate)
-        w = residue[:, lanes(c)] * jnp.sqrt(one_minus_exp(2.0 * rate))
-        decay[c] = a
+        decay[c] = jnp.exp(-rate)
         seg_decay[c] = jnp.exp(rate * (-float(seg)))
         dev_decay[c] = jnp.exp(rate * (-float(length)))
-        power = w
+        carry[0, c] = jnp.zeros((modes, LANES), jnp.float32)
+        carry[1, c] = jnp.zeros((modes, LANES), jnp.float32)
+
+    def filters(c):
+        a = decay[c]
+        power = residue[:, lanes(c)] * jnp.sqrt(one_minus_exp(2.0 * rates[:, lanes(c)]))
         for k in range(seg):
             tap = jnp.sum(power, axis=0, keepdims=True)
             if k == 0:
@@ -164,10 +196,10 @@
             power = power * a
             if k == 0:
                 weight[c] = power
-        carry[0, c] = jnp.zeros((modes, LANES), jnp.float32)
-        carry[1, c] = jnp.zeros((modes, LANES), jnp.float32)
-
+
+    loads[1].wait()
     each(prepare)
+    loads[2].wait()
 
     @pl.when(me > 0)
     def _():
@@ -212,26 +244,27 @@
     def comes(d, k):
         return me >= 2**k if d == 0 else me + 2**k < n_ctx
 
-    def carry_copy(d, k):
+    def carry_copy(d, k, g):
+        some = pl.ds(g * per, per)
         to = me + 2**k if d == 0 else me - 2**k
         return pltpu.make_async_remote_copy(
-            src_ref=sent.at[d, k],
-            dst_ref=landed.at[d, k],
-            send_sem=carry_send.at[d, k],
-            recv_sem=carry_recv.at[d, k],
+            src_ref=sent.at[d, k, some],
+            dst_ref=landed.at[d, k, some],
+            send_sem=carry_send.at[d, k, g],
+            recv_sem=carry_recv.at[d, k, g],
             device_id=(jnp.clip(to, 0, n_ctx - 1), mine),
             device_id_type=pl.DeviceIdType.MESH,
         )
 
-    def send(d, k):
+    def send(d, k, g):
         @pl.when(reach(d, k))
         def _():
-            carry_copy(d, k).start()
-
-    def take(d, k):
+            carry_copy(d, k, g).start()
+
+    def take(d, k, g):
         @pl.when(comes(d, k))
         def _():
-            carry_copy(d, k).wait_recv()
+            carry_copy(d, k, g).wait_recv()
 
             def add(c):
                 arrived = landed[d, k, c]
@@ -239,7 +272,7 @@
                     arrived = arrived * jnp.exp(rates[:, lanes(c)] * (-float(length * (2**k - 1))))
                 carry[d, c] = carry[d, c] + arrived
 
-            each(add)
+            within(g, add)
 
         if k + 1 < rounds:
 
@@ -248,8 +281,8 @@
                 def join(c):
                     sent[d, k + 1, c] = sent[d, 0, c] + dev_decay[c] * carry[d, c]
 
-                each(join)
-                carry_copy(d, k + 1).start()
+                within(g, join)
+                carry_copy(d, k + 1, g).start()
 
     def forward_ends(c):
         for x in range(3):
@@ -261,9 +294,15 @@
             values[c, j] = v_now[j]
         ends([k_now[j] * v_now[j] for j in range(seg)], c, False)
 
-    each(forward_ends)
-    if rounds:
-        send(0, 0)
+    def forward_ends_group(g):
+        within(g, forward_ends)
+        if rounds:
+            send(0, 0, g)
+
+    loop(group, forward_ends_group)
+    loads[3].wait()
+    loads[4].wait()
+    each(filters)
 
     own.wait()
     for copy in row_copies:
@@ -279,10 +318,13 @@
             signal.append(now)
         ends(signal, c, True)
 
-    each(backward_ends)
-    if rounds:
-        send(1, 0)
-        take(0, 0)
+    def backward_ends_group(g):
+        within(g, backward_ends)
+        if rounds:
+            send(1, 0, g)
+            take(0, 0, g)
+
+    loop(group, backward_ends_group)
 
     def forward_short(c):
         h = [wide(short[c, k : k + 1, :]) for k in range(seg)]
@@ -293,11 +335,14 @@
                 total = total + h[k] * p[j - k]
             partial[0, c, j] = total
 
-    each(forward_short)
-    if rounds:
-        take(1, 0)
-    if rounds > 1:
-        take(0, 1)
+    def forward_short_group(g):
+        within(g, forward_short)
+        if rounds:
+            take(1, 0, g)
+        if rounds > 1:
+            take(0, 1, g)
+
+    loop(group, forward_short_group)
 
     def backward_short(c):
         h = [wide(short[c, k : k + 1, :]) for k in range(seg)]
@@ -308,13 +353,19 @@
                 total = total + h[k] * p[j + k]
             partial[1, c, j] = total
 
-    each(backward_short)
-    if rounds > 1:
-        take(1, 1)
-    for k in range(2, rounds):
-        take(0, k)
-        if k + 1 < rounds:
-            take(1, k)
+    def backward_short_group(g):
+        within(g, backward_short)
+        if rounds > 1:
+            take(1, 1, g)
+
+    loop(group, backward_short_group)
+    for k in range(2, rounds - 1):
+
+        def both(g):
+            take(0, k, g)
+            take(1, k, g)
+
+        loop(group, both)
 
     def complete(c, d):
         a = [wide(decay[c, m : m + 1, :]) for m in range(modes)]
@@ -340,9 +391,12 @@
         for j in range(seg):
             stream[0, c, j] = conv[j] * g32[c, pl.ds(j, SEGS, stride=seg), :]
 
-    each(forward_finish)
-    if rounds > 2:
-        take(1, rounds - 1)
+    def forward_finish_group(g):
+        if rounds > 2:
+            take(0, rounds - 1, g)
+        within(g, forward_finish)
+
+    loop(group, forward_finish_group)
 
     def rim_copy(g):
         some = pl.ds(g * per, per)
@@ -365,20 +419,16 @@
             for r in range(2):
                 rim_out[c, 2 * x + r : 2 * x + r + 1, :] = stream[x, c, r, 0:1, :]
 
-    def finish_group(g, _):
-        def one(i, _):
-            backward_finish(g * per + i)
-            return 0
-
-        lax.fori_loop(0, per, one, 0)
+    def backward_finish_group(g):
+        if rounds > 2:
+            take(1, rounds - 1, g)
+        within(g, backward_finish)
 
         @pl.when(me > 0)
         def _():
             rim_copy(g).start()
 
-        return 0
-
-    lax.fori_loop(0, group, finish_group, 0)
+    loop(group, backward_finish_group)
 
     @pl.when(me == n_ctx - 1)
     def _():
@@ -395,19 +445,14 @@
                 placed[x, pl.ds(j, SEGS, stride=seg), :] = t[0] * g[j] + t[1] * g[j + 1] + t[2] * g[j + 2]
             out[x, :, lanes(c)] = placed[x].astype(out.dtype)
 
-    def output_group(g, _):
+    def output_group(g):
         @pl.when(me < n_ctx - 1)
         def _():
             rim_copy(g).wait_recv()
 
-        def one(i, _):
-            last_taps(g * per + i)
-            return 0
-
-        lax.fori_loop(0, per, one, 0)
-        return 0
-
-    lax.fori_loop(0, group, output_group, 0)
+        within(g, last_taps)
+
+    loop(group, output_group)
 
     @pl.when(me < n_ctx - 1)
     def _():
@@ -418,15 +463,11 @@
 
             @pl.when(reach(d, k))
             def _():
-                carry_copy(d, k).wait_send()
+                loop(group, lambda g: carry_copy(d, k, g).wait_send())
 
     @pl.when(me > 0)
     def _():
-        def drain(g, _):
-            rim_copy(g).wait_send()
-            return 0
-
-        lax.fori_loop(0, group, drain, 0)
+        loop(group, lambda g: rim_copy(g).wait_send())
 
 
 def per_device(n_ctx, n_ch, features, grad_rows, conv_taps, decay_rate, residue, skip_gain):
@@ -445,9 +486,14 @@
     return pl.pallas_call(
         functools.partial(kernel, n_ctx, n_ch),
         out_shape=jax.ShapeDtypeStruct(features.shape, jnp.bfloat16),
-        in_specs=[vmem] * 6,
+        in_specs=[pl.BlockSpec(memory_space=pl.ANY)] * 6,
         out_specs=vmem,
         scratch_shapes=[
+            pltpu.VMEM(features.shape, features.dtype),
+            pltpu.VMEM(conv_taps.shape, f32),
+            pltpu.VMEM(decay_rate.shape, f32),
+            pltpu.VMEM(residue.shape, f32),
+            pltpu.VMEM((1, width), f32),
             pltpu.VMEM((3, tiles, 8 + length, LANES), f32),
             pltpu.VMEM((length, width), jnp.bfloat16),
             pltpu.VMEM((tiles, length, LANES), f32),
@@ -470,18 +516,19 @@
             edge,
             edge,
             pltpu.VMEM((3, length, LANES), f32),
+            dma((5,)),
             dma,
             dma((n_ch - 1,)),
             dma((n_ch - 1,)),
             dma,
             dma,
-            dma((2, rounds)),
-            dma((2, rounds)),
+            dma((2, rounds, group)),
+            dma((2, rounds, group)),
             dma((group,)),
             dma((group,)),
         ],
         compiler_params=pltpu.CompilerParams(
-            collective_id=0, has_side_effects=True, vmem_limit_bytes=48 * 1024 * 1024
+            collective_id=0, has_side_effects=True, vmem_limit_bytes=56 * 1024 * 1024
         ),
     )(features, grad_rows, conv_taps, decay_rate, residue, skip_gain[None])
 

time: 42.5 us -> 35.6 us (0.84)
  local copies, waits for them, and re-layouts: 6.99 us -> 2.73 us
  Pallas kernels: 35.2 us -> 32.7 us
    unnamed x13 -> x1, local copies, waits for them, and re-layouts: 6.99 us -> 2.73 us
    pallas_call x1, Pallas kernels: 35.2 us -> 32.7 us  [per_device(): pl.pallas_call(functools.partial(kernel, n_ctx, n_ch), out_shape=jax.Shap...]
where the time goes in v2:
time: 35.6 us; the launch traced here: 35.4 us
  Pallas kernels  32.7 us (92%)
  local copies, waits for them, and re-layouts  2.73 us (8%)
    pallas_call x1, Pallas kernels, per_device(): pl.pallas_call(functools.partial(kernel, n_ctx, n_ch), out_shape=jax.Shap...  32.7 us
    unnamed x1, local copies, waits for them, and re-layouts  2.73 us

profile of v2, /device:TPU:0, one launch (start us, length us, event | category | flops | bytes accessed | tf_op | source)
XLA Modules:
  0.0 35.4 jit_solution(16736954819984086368)
XLA Ops:
  0.0 32.7 %shard_map.64 = bf16[3,128,2048]{2,1,0:T(8,128)(2,1)} custom-call(bf16[3,128,2048]{2,1,0:T(8,128)(2,1)} %features_hbm.1, bf16[32,8192]{1,0:T(8,128)(2,1)} %rows.1, f32[3,3,2048]{2,1,0:T(4,128)} %taps_hbm.1, f32[16,2048]{1,0:T(8,128)} %rates_hbm.1, f32[16,2048]{1,0:T(8,128)} %residue_hbm.1, f32[1,2048]{1,0:T(1,128)} %bitcast.1), custom_call_target="tpu_custom_call" | custom-call | tf_op jit(solution)/shard_map/pallas_call | solution.py:486
  32.7 2.7 %copy.8 = bf16[3,128,2048]{2,1,0:T(8,128)(2,1)} copy(bf16[3,128,2048]{2,1,0:T(8,128)(2,1)} %shard_map.64) | data formatting | bytes 3145728

commit v3 on v2

--- a/solution.py
+++ b/solution.py
@@ -16,6 +16,15 @@
     for k in range(10, 1, -1):
         series = 1.0 - x * (1.0 / k) * series
     return jnp.where(x < 0.5, x * series, 1.0 - jnp.exp(-x))
+
+
+def added(terms):
+    sums = list(terms[:4])
+    for i, term in enumerate(terms[4:]):
+        sums[i % 4] = sums[i % 4] + term
+    while len(sums) > 1:
+        sums = [sums[i] + sums[i + 1] if i + 1 < len(sums) else sums[i] for i in range(0, len(sums), 2)]
+    return sums[0]
 
 
 def kernel(
@@ -330,10 +339,7 @@
         h = [wide(short[c, k : k + 1, :]) for k in range(seg)]
         p = [keys[c, j] * values[c, j] for j in range(seg)]
         for j in range(seg):
-            total = h[0] * p[j]
-            for k in range(1, j + 1):
-                total = total + h[k] * p[j - k]
-            partial[0, c, j] = total
+            partial[0, c, j] = added([h[k] * p[j - k] for k in range(j + 1)])
 
     def forward_short_group(g):
         within(g, forward_short)
@@ -348,10 +354,7 @@
         h = [wide(short[c, k : k + 1, :]) for k in range(seg)]
         p = [gconv[c, j] for j in range(seg)]
         for j in range(seg):
-            total = h[0] * p[j]
-            for k in range(1, seg - j):
-                total = total + h[k] * p[j + k]
-            partial[1, c, j] = total
+            partial[1, c, j] = added([h[k] * p[j + k] for k in range(seg - j)])
 
     def backward_short_group(g):
         within(g, backward_short)
@@ -378,12 +381,9 @@
         result = [None] * seg
         order = range(seg - 1, -1, -1) if d else range(seg)
         for step, j in enumerate(order):
-            total = partial[d, c, j]
             if step:
                 y = [y[m] * a[m] for m in range(modes)]
-            for m in range(modes):
-                total = total + y[m]
-            result[j] = total
+            result[j] = partial[d, c, j] + added(y)
         return result
 
     def forward_finish(c):

time: 35.6 us -> 35.5 us (level)
  no operation moved by 1% of the time
where the time goes in v3:
time: 35.5 us; the launch traced here: 35.4 us
  Pallas kernels  32.6 us (92%)
  local copies, waits for them, and re-layouts  2.73 us (8%)
    pallas_call x1, Pallas kernels, per_device(): pl.pallas_call(functools.partial(kernel, n_ctx, n_ch), out_shape=jax.Shap...  32.6 us
    unnamed x1, local copies, waits for them, and re-layouts  2.73 us

profile of v3, /device:TPU:0, one launch (start us, length us, event | category | flops | bytes accessed | tf_op | source)
XLA Modules:
  0.0 35.4 jit_solution(9197101639841983291)
XLA Ops:
  0.0 32.6 %shard_map.64 = bf16[3,128,2048]{2,1,0:T(8,128)(2,1)} custom-call(bf16[3,128,2048]{2,1,0:T(8,128)(2,1)} %features_hbm.1, bf16[32,8192]{1,0:T(8,128)(2,1)} %rows.1, f32[3,3,2048]{2,1,0:T(4,128)} %taps_hbm.1, f32[16,2048]{1,0:T(8,128)} %rates_hbm.1, f32[16,2048]{1,0:T(8,128)} %residue_hbm.1, f32[1,2048]{1,0:T(1,128)} %bitcast.1), custom_call_target="tpu_custom_call" | custom-call | tf_op jit(solution)/shard_map/pallas_call | solution.py:486
  32.6 2.7 %copy.8 = bf16[3,128,2048]{2,1,0:T(8,128)(2,1)} copy(bf16[3,128,2048]{2,1,0:T(8,128)(2,1)} %shard_map.64) | data formatting | bytes 3145728
